TPU v7x, 32 devices: a whole 2x2x4 slice. The times are simulated.
32 devices in a mesh: grp: 2 (over y), gx: 16 (over z, x, core).
Axes of the slice: x: 2, y: 2, z: 4, core: 2. Of those that a mesh axis runs over, the one named last changes fastest.
Arguments:
- features: bfloat16 [128, 32, 64, 128], P('grp', 'gx'), parts along dimension 0, may hold values from -6 to 6
- cotangent: bfloat16 [128, 32, 64, 128], P('grp', 'gx'), parts along dimension 0, may hold values from -6 to 6
- spectral_weight: bfloat16 [16384, 64, 128], P('gx'), may hold values from -0.5 to 0.5
- channel_weight: bfloat16 [64, 64], replicated, may hold values from -0.75 to 0.75
- channel_bias: float32 [64], replicated, may hold values from -3 to 3
Outputs:
- activated: bfloat16 [128, 32, 64, 128], P('grp', 'gx'), parts along dimension 0
- feature_grad: bfloat16 [128, 32, 64, 128], P('grp', 'gx'), parts along dimension 0
- spectral_grad: bfloat16 [32768, 64, 128], P(('grp', 'gx')), parts along dimension 0
There are 2 independent parts, one for each index of `grp`. A program takes and returns all parts, laid end to end along the dimension named above; an argument that names none is the same for every part. Nothing has to cross between parts.
All inputs are finite; a program needn't handle non-finite values.
Results may differ from a plain program's by a relative error of at most 0.018.
Values may be sent and summed in bfloat16 or wider, within the bound.
A program may use at most 192 MiB of HBM per device.

v0:
```python
import functools
import math

import jax
import jax.numpy as jnp
from jax import lax
from jax.experimental import pallas as pl
from jax.experimental.pallas import tpu as pltpu
from jax.sharding import PartitionSpec as P

MX = 32
MY = 32
MZ = 16


SQRT_TWO_PI = math.sqrt(2.0 / math.pi)
CUBIC_COEF = 0.044715


def freq_index(retained, length):
    ladder = jnp.arange(retained, dtype=jnp.int32)
    return jnp.where(ladder < retained // 2, ladder, length - retained + ladder)


def cos_sin(wavenum, length):
    points = jnp.arange(length, dtype=jnp.int32)
    angles = (wavenum[:, None] * points[None, :] % length).astype(jnp.float32) * (
        2.0 * math.pi / length
    )
    return (jnp.cos(angles), jnp.sin(angles))


def analysis_pair(wavenum, length):
    cosine, sine_wave = cos_sin(wavenum, length)
    cosine, sine_wave = (cosine.T, sine_wave.T)
    return jnp.stack(
        [jnp.stack([cosine, -sine_wave], 1), jnp.stack([sine_wave, cosine], 1)], 1
    ).astype(jnp.bfloat16)


def synthesis_pair(wavenum, length):
    cosine, sine_wave = cos_sin(wavenum, length)
    return jnp.stack(
        [jnp.stack([cosine, sine_wave], 1), jnp.stack([-sine_wave, cosine], 1)], 1
    ).astype(jnp.bfloat16)


def depth_table(retained, length):
    cosine, sine_wave = cos_sin(jnp.arange(retained, dtype=jnp.int32), length)
    return jnp.concatenate([cosine, -sine_wave], 0).astype(jnp.bfloat16)


def gelu_parts(inputs):
    cubed_in = inputs * inputs * inputs
    tangent = jnp.tanh(SQRT_TWO_PI * (inputs + CUBIC_COEF * cubed_in))
    output = 0.5 * inputs * (1.0 + tangent)
    derivative = 0.5 * (1.0 + tangent) + 0.5 * inputs * (1.0 - tangent * tangent) * SQRT_TWO_PI * (
        1.0 + 3.0 * CUBIC_COEF * inputs * inputs
    )
    return (output, derivative)


def mode_product(coeffs, weights):
    channels = weights.shape[1]
    halves = jnp.einsum("mac,mcj->amj", coeffs, weights, preferred_element_type=jnp.float32)
    real_out = halves[0, :, :channels] - halves[1, :, channels:]
    imag_out = halves[0, :, channels:] + halves[1, :, :channels]
    return jnp.stack([real_out, imag_out], 1).astype(jnp.bfloat16)


def exchange(blocks):
    return lax.all_to_all(blocks, "gx", 0, 0, tiled=True)


def middle_kernel(
    scale, feat_ref, cot_ref, lines_ref, weight_ref, bias_ref, basis_ref, act_ref, up_ref, grad_ref
):
    channels, _, rows, depth_len = feat_ref.shape
    spectral = jnp.dot(
        lines_ref[0].reshape(rows * channels, lines_ref.shape[3]),
        basis_ref[...],
        preferred_element_type=jnp.float32,
    ).reshape(rows, channels, depth_len)
    feats = jnp.swapaxes(feat_ref[:, 0].astype(jnp.float32), 0, 1).astype(jnp.bfloat16)
    cots = jnp.swapaxes(cot_ref[:, 0].astype(jnp.float32), 0, 1)
    acts = []
    for row in range(rows):
        pointwise = jnp.dot(weight_ref[...], feats[row], preferred_element_type=jnp.float32)
        hidden = spectral[row] * scale + pointwise + bias_ref[...]
        activated, derivative = gelu_parts(hidden)
        acts.append(activated)
        up_ref[0, row] = (cots[row] * derivative).astype(jnp.bfloat16)
    act_ref[:, 0] = jnp.swapaxes(jnp.stack(acts, 0), 0, 1).astype(jnp.bfloat16)
    grad = lax.dot_general(
        up_ref[0].reshape(rows * channels, depth_len),
        basis_ref[...],
        (((1,), (1,)), ((), ())),
        preferred_element_type=jnp.float32,
    )
    grad_ref[0] = (grad * scale).astype(jnp.bfloat16).reshape(rows, channels, lines_ref.shape[3])


def final_kernel(up_ref, depth_ref, weight_ref, basis_ref, out_ref):
    _, rows, channels, depth_len = up_ref.shape
    spectral = jnp.dot(
        depth_ref[0].reshape(rows * channels, depth_ref.shape[3]),
        basis_ref[...],
        preferred_element_type=jnp.float32,
    ).reshape(rows, channels, depth_len)
    totals = []
    for row in range(rows):
        back = jnp.dot(weight_ref[...], up_ref[0, row], preferred_element_type=jnp.float32)
        totals.append(spectral[row] + back)
    out_ref[:, 0] = jnp.swapaxes(jnp.stack(totals, 0), 0, 1).astype(jnp.bfloat16)


ROWS = 16


def middle(features, cotangent, lines_back, channel_weight, channel_bias, depth_basis, scale):
    channels, planes, lines, depth_len = features.shape
    parts = lines_back.shape[3]
    field = pl.BlockSpec((channels, 1, ROWS, depth_len), lambda x, y: (0, x, y, 0))
    turned = pl.BlockSpec((1, ROWS, channels, depth_len), lambda x, y: (x, y, 0, 0))
    narrow = pl.BlockSpec((1, ROWS, channels, parts), lambda x, y: (x, y, 0, 0))
    count = features.size
    return pl.pallas_call(
        functools.partial(middle_kernel, scale),
        grid=(planes, lines // ROWS),
        in_specs=[
            field,
            field,
            narrow,
            pl.BlockSpec((channels, channels), lambda x, y: (0, 0)),
            pl.BlockSpec((channels, 1), lambda x, y: (0, 0)),
            pl.BlockSpec((parts, depth_len), lambda x, y: (0, 0)),
        ],
        out_specs=[field, turned, narrow],
        out_shape=[
            jax.ShapeDtypeStruct(features.shape, jnp.bfloat16),
            jax.ShapeDtypeStruct((planes, lines, channels, depth_len), jnp.bfloat16),
            jax.ShapeDtypeStruct((planes, lines, channels, parts), jnp.bfloat16),
        ],
        compiler_params=pltpu.CompilerParams(vmem_limit_bytes=56 * 1024 * 1024),
        cost_estimate=pl.CostEstimate(
            flops=count * 2 * (channels + 2 * parts), bytes_accessed=count * 8, transcendentals=count
        ),
    )(features, cotangent, lines_back, channel_weight, channel_bias[:, None], depth_basis)


def final(upstream, depth_grad, weight_back, depth_basis):
    planes, lines, channels, depth_len = upstream.shape
    parts = depth_grad.shape[3]
    count = upstream.size
    return pl.pallas_call(
        final_kernel,
        grid=(planes, lines // ROWS),
        in_specs=[
            pl.BlockSpec((1, ROWS, channels, depth_len), lambda x, y: (x, y, 0, 0)),
            pl.BlockSpec((1, ROWS, channels, parts), lambda x, y: (x, y, 0, 0)),
            pl.BlockSpec((channels, channels), lambda x, y: (0, 0)),
            pl.BlockSpec((parts, depth_len), lambda x, y: (0, 0)),
        ],
        out_specs=pl.BlockSpec((channels, 1, ROWS, depth_len), lambda x, y: (0, x, y, 0)),
        out_shape=jax.ShapeDtypeStruct((channels, planes, lines, depth_len), jnp.bfloat16),
        compiler_params=pltpu.CompilerParams(vmem_limit_bytes=32 * 1024 * 1024),
        cost_estimate=pl.CostEstimate(
            flops=count * 2 * (channels + parts), bytes_accessed=count * 4, transcendentals=0
        ),
    )(upstream, depth_grad, weight_back, depth_basis)


def body(features, cotangent, spectral_weight, channel_weight, channel_bias):
    channels, planes, lines, depth_len = features.shape
    devices = lax.axis_size("gx")
    all_planes = planes * devices
    owned_modes = spectral_weight.shape[0]
    wave_pairs = MY * MZ
    owned_pairs = owned_modes // MX
    wide = 2 * channels
    forward_scale = 1.0 / math.sqrt(all_planes * lines * depth_len)
    inverse_scale = 1.0 / math.sqrt(MX * wave_pairs)
    weight_scale = math.sqrt(MX * wave_pairs / (all_planes * lines * depth_len))
    depth_basis = depth_table(MZ, depth_len)
    across_y = analysis_pair(freq_index(MY, lines), lines)
    back_y = synthesis_pair(freq_index(MY, lines), lines)
    across_x = analysis_pair(freq_index(MX, all_planes), all_planes)
    back_x = synthesis_pair(freq_index(MX, all_planes), all_planes)

    def to_owners(rows):
        blocks = rows.reshape(devices, owned_pairs * planes, wide)
        return exchange(blocks).reshape(devices, owned_pairs, planes, 2, channels)

    def to_planes(rows):
        blocks = rows.reshape(devices, planes * owned_pairs, wide)
        got = exchange(blocks).reshape(devices, planes, owned_pairs, 2, channels)
        return got.transpose(1, 0, 2, 3, 4).reshape(planes, MY, MZ, 2, channels)

    depth_part = jnp.dot(features, depth_basis.T, preferred_element_type=jnp.float32).astype(
        jnp.bfloat16
    )
    plane_part = jnp.einsum(
        "cxyaz,yabk->kzxbc",
        depth_part.reshape(channels, planes, lines, 2, MZ),
        across_y,
        preferred_element_type=jnp.float32,
    ).astype(jnp.bfloat16)
    gathered = to_owners(plane_part)
    mode_sums = jnp.einsum(
        "sqpac,spabk->qkbc",
        gathered,
        across_x.reshape(devices, planes, 2, 2, MX),
        preferred_element_type=jnp.float32,
    )
    coeffs = (mode_sums * forward_scale).astype(jnp.bfloat16).reshape(owned_modes, 2, channels)
    spectral = mode_product(coeffs, spectral_weight)
    planes_back = jnp.einsum(
        "qkao,kabx->xqbo",
        spectral.reshape(owned_pairs, MX, 2, channels),
        back_x,
        preferred_element_type=jnp.float32,
    ).astype(jnp.bfloat16)
    planes_here = to_planes(planes_back)
    lines_back = (
        jnp.einsum("xkzao,kaby->xyobz", planes_here, back_y, preferred_element_type=jnp.float32)
        .astype(jnp.bfloat16)
        .reshape(planes, lines, channels, 2 * MZ)
    )
    activated, upstream, lines_grad = middle(
        features, cotangent, lines_back, channel_weight, channel_bias, depth_basis, inverse_scale
    )
    rows_grad = jnp.einsum(
        "xyobz,kaby->kzxao",
        lines_grad.reshape(planes, lines, channels, 2, MZ),
        back_y,
        preferred_element_type=jnp.float32,
    ).astype(jnp.bfloat16)
    gathered_grad = to_owners(rows_grad)
    grad_modes = (
        jnp.einsum(
            "sqpbo,kabsp->qkao",
            gathered_grad,
            back_x.reshape(MX, 2, 2, devices, planes),
            preferred_element_type=jnp.float32,
        )
        .astype(jnp.bfloat16)
        .reshape(owned_modes, 2, channels)
    )
    straight = grad_modes.reshape(owned_modes, wide)
    rotated = jnp.concatenate([grad_modes[:, 1], -grad_modes[:, 0]], 1)
    pairs = jnp.stack([straight, rotated], 1)
    coeff_grad = (
        jnp.einsum("mcj,mbj->mbc", spectral_weight, pairs, preferred_element_type=jnp.float32)
        * forward_scale
    ).astype(jnp.bfloat16)
    plane_grad = jnp.einsum(
        "qkbc,xabk->xqac",
        coeff_grad.reshape(owned_pairs, MX, 2, channels),
        across_x,
        preferred_element_type=jnp.float32,
    ).astype(jnp.bfloat16)
    grad_here = to_planes(plane_grad)
    spectral_grad = (
        jnp.einsum("mac,maj->mcj", coeffs, pairs, preferred_element_type=jnp.float32)
        * weight_scale
    ).astype(jnp.bfloat16)
    depth_grad = (
        jnp.einsum("xkzbc,yabk->xycaz", grad_here, across_y, preferred_element_type=jnp.float32)
        .astype(jnp.bfloat16)
        .reshape(planes, lines, channels, 2 * MZ)
    )
    feature_grad = final(upstream, depth_grad, channel_weight.T, depth_basis)
    return (activated, feature_grad, spectral_grad)


def solution(mesh):
    in_specs = (
        P("grp", "gx", None, None),
        P("grp", "gx", None, None),
        P("gx", None, None),
        P(),
        P(),
    )
    out_specs = (
        P("grp", "gx", None, None),
        P("grp", "gx", None, None),
        P(("grp", "gx"), None, None),
    )
    return jax.shard_map(body, mesh=mesh, in_specs=in_specs, out_specs=out_specs, check_vma=False)
```

profile of v0, /device:TPU:0, one launch (start us, length us, event | category | flops | bytes accessed | tf_op | source)
XLA Modules:
  0.0 122.4 jit_solution(15389460319423207074)
XLA Ops:
  0.7 0.2 negate_convert_fusion.1
  0.9 3.7 %convolution_convert_fusion = bf16[32,64,2,64]{3,0,2,1:T(8,128)(2,1)S(1)} fusion(bf16[64,2,64,128]{3,2,1,0:T(8,128)(2,1)} %feat_ref.1, bf16[16,128]{1,0:T(8,128)(2,1)S(1)} %get-tuple-element.35, bf16[16,128]{1,0:T(8,128)(2,1)S(1)} %get-tuple-element.36), kind=kOutput, calls=%fused_computation.3 | convolution fusion | flops 67387392 | bytes 2629632 | tf_op jit(solution)/shard_map/dot_general | solution.py:199
  4.5 1.4 %fusion.13 = bf16[32,16,2,2,64]{4,0,1,2,3:T(8,128)(2,1)S(1)} fusion(bf16[64,2,64,2,16]{2,4,3,1,0:T(8,128)(2,1)S(1)} %bitcast.196, bf16[64,1,2,32]{0,3,1,2:T(8,128)(2,1)S(1)} %get-tuple-element.22, bf16[64,1,2,32]{0,3,1,2:T(8,128)(2,1)S(1)} %get-tuple-element.21), kind=kOutput, calls=%fused_computation.25 | convolution fusion | flops 33718272 | bytes 802816 | tf_op jit(solution)/shard_map/cxyaz,yabk->kzxbc/dot_general | solution.py:202
  5.9 0.5 copy.29
  6.5 1.0 reshape.548
  7.4 7.4 %all-to-all-start = ((bf16[16,64,128]{2,1,0:T(8,128)(2,1)}), bf16[16,64,128]{2,1,0:T(8,128)(2,1)S(1)}, u32[]{:S(2)}, u32[]{:S(2)}) async-start(bf16[16,64,128]{2,1,0:T(8,128)(2,1)} %reshape.548), calls=%async_computation | async-start | bytes 524288 | tf_op jit(solution)/shard_map/all_to_all | solution.py:72
  15.2 9.7 %all-to-all-done = bf16[16,64,128]{2,1,0:T(8,128)(2,1)S(1)} async-done(((bf16[16,64,128]{2,1,0:T(8,128)(2,1)}), bf16[16,64,128]{2,1,0:T(8,128)(2,1)S(1)}, u32[]{:S(2)}, u32[]{:S(2)}) %all-to-all-start) | async-done | bytes 262176 | tf_op jit(solution)/shard_map/all_to_all | solution.py:72
  24.8 0.2 reshape.549
  25.1 0.5 fusion.3
  25.6 8.1 %convolution_bitcast_fusion.5 = f32[2,1024,128]{2,0,1:T(2,128)S(1)} fusion(bf16[1024,64,128]{2,1,0:T(8,128)(2,1)} %param.7, bf16[1024,2,64]{2,0,1:T(8,128)(2,1)S(1)} %bitcast.199), kind=kOutput, calls=%fused_computation.11 | convolution fusion | flops 33554432 | bytes 18087936 | tf_op jit(solution)/shard_map/mac,mcj->amj/dot_general | solution.py:65
  33.7 2.3 %fusion.19 = (bf16[1,1024,64]{2,0,1:T(2,128)(2,1)S(1)}, bf16[1,1024,64]{2,0,1:T(2,128)(2,1)S(1)}) fusion(f32[2,1024,128]{2,0,1:T(2,128)S(1)} %convolution_bitcast_fusion.5), kind=kLoop, calls=%fused_computation.33 | loop fusion | flops 262144 | bytes 1310720 | tf_op jit(solution)/shard_map/convert.17
  36.2 0.3 fusion.11
  36.5 0.5 copy.34
  37.1 1.0 reshape.551
  38.0 3.7 %all-to-all-start.1 = ((bf16[16,64,128]{2,1,0:T(8,128)(2,1)}), bf16[16,64,128]{2,1,0:T(8,128)(2,1)S(1)}, u32[]{:S(2)}, u32[]{:S(2)}) async-start(bf16[16,64,128]{2,1,0:T(8,128)(2,1)} %reshape.551), calls=%async_computation.1 | async-start | bytes 524288 | tf_op jit(solution)/shard_map/all_to_all | solution.py:72
  41.8 0.7 copy.39.bias_ref
  42.5 0.6 pad_maximum_fusion.9.basis_ref
  43.2 8.4 %all-to-all-done.1 = bf16[16,64,128]{2,1,0:T(8,128)(2,1)S(1)} async-done(((bf16[16,64,128]{2,1,0:T(8,128)(2,1)}), bf16[16,64,128]{2,1,0:T(8,128)(2,1)S(1)}, u32[]{:S(2)}, u32[]{:S(2)}) %all-to-all-start.1) | async-done | bytes 262176 | tf_op jit(solution)/shard_map/all_to_all | solution.py:72
  51.6 0.2 reshape.552
  51.9 0.5 fusion
  52.4 0.7 copy.37
  53.1 1.8 %copy.38.lines_ref = bf16[2,64,64,32]{3,2,1,0:T(8,128)(2,1)} copy(bf16[2,64,64,32]{2,3,1,0:T(8,128)(2,1)S(1)} %bitcast.197) | data formatting | bytes 1048576 | tf_op jit(solution)/shard_map/reshape | solution.py:227
  54.9 11.4 %shard_map.76 = (bf16[64,2,64,128]{3,2,1,0:T(8,128)(2,1)}, bf16[2,64,64,128]{3,2,1,0:T(8,128)(2,1)}, bf16[2,64,64,32]{3,2,1,0:T(8,128)(2,1)}) custom-call(bf16[64,2,64,128]{3,2,1,0:T(8,128)(2,1)} %feat_ref.1, bf16[64,2,64,128]{3,2,1,0:T(8,128)(2,1)} %cot_ref.1, bf16[2,64,64,32]{3,2,1,0:T(8,128)(2,1)} %copy.38.lines_ref, bf16[64,64]{1,0:T(8,128)(2,1)} %weight_ref.1, ...), custom_call_target="tpu_custom_call" | custom-call | flops 268435456 | bytes 8388608 | tf_op jit(solution)/shard_map/pallas_call | solution.py:127
  66.3 2.0 %copy.40 = bf16[2,64,64,32]{2,3,1,0:T(8,128)(2,1)S(1)} copy(bf16[2,64,64,32]{3,2,1,0:T(8,128)(2,1)} %get-tuple-element.8) | data formatting | bytes 1048576 | tf_op jit(solution)/shard_map/pallas_call | solution.py:127
  68.3 0.5 fusion.12
  68.8 0.5 copy.43
  69.3 1.0 reshape.556
  70.3 3.5 %all-to-all-start.2 = ((bf16[16,64,128]{2,1,0:T(8,128)(2,1)}), bf16[16,64,128]{2,1,0:T(8,128)(2,1)S(1)}, u32[]{:S(2)}, u32[]{:S(2)}) async-start(bf16[16,64,128]{2,1,0:T(8,128)(2,1)} %reshape.556), calls=%async_computation.2 | async-start | bytes 524288 | tf_op jit(solution)/shard_map/all_to_all | solution.py:72
  73.9 0.2 fusion.96
  74.1 9.7 %all-to-all-done.2 = bf16[16,64,128]{2,1,0:T(8,128)(2,1)S(1)} async-done(((bf16[16,64,128]{2,1,0:T(8,128)(2,1)}), bf16[16,64,128]{2,1,0:T(8,128)(2,1)S(1)}, u32[]{:S(2)}, u32[]{:S(2)}) %all-to-all-start.2) | async-done | bytes 262176 | tf_op jit(solution)/shard_map/all_to_all | solution.py:72
  83.8 0.2 reshape.557
  84.1 0.5 fusion.5
  84.6 0.5 copy.45
  85.2 0.3 stack_reshape_reshape.4
  85.7 0.4 copy.47
  86.1 12.3 %fusion.7 = bf16[1024,2,64]{2,1,0:T(2,128)(2,1)S(1)} fusion(bf16[1024,64,128]{2,1,0:T(8,128)(2,1)} %param.7, bf16[1024,1,128]{2,1,0:T(2,128)(2,1)S(1)} %copy.47, bf16[1024,1,128]{2,1,0:T(2,128)(2,1)S(1)} %stack_reshape_reshape.4), kind=kOutput, calls=%fused_computation.19 | convolution fusion | flops 34865152 | bytes 17563648 | tf_op jit(solution)/shard_map/mcj,mbj->mbc/dot_general | solution.py:253
  98.4 0.3 fusion.10
  98.8 0.5 copy.50
  99.3 1.0 reshape.560
  100.3 3.8 %all-to-all-start.3 = ((bf16[16,64,128]{2,1,0:T(8,128)(2,1)}), bf16[16,64,128]{2,1,0:T(8,128)(2,1)S(1)}, u32[]{:S(2)}, u32[]{:S(2)}) async-start(bf16[16,64,128]{2,1,0:T(8,128)(2,1)} %reshape.560), calls=%async_computation.3 | async-start | bytes 524288 | tf_op jit(solution)/shard_map/all_to_all | solution.py:72
  104.0 9.5 %multiply_convert_fusion = bf16[1024,64,128]{2,1,0:T(8,128)(2,1)} fusion(bf16[1024,2,64]{2,0,1:T(8,128)(2,1)S(1)} %bitcast.200, bf16[1024,1,128]{2,1,0:T(2,128)(2,1)S(1)} %copy.47, bf16[1024,1,128]{2,1,0:T(2,128)(2,1)S(1)} %stack_reshape_reshape.4), kind=kOutput, calls=%fused_computation | convolution fusion | flops 51380224 | bytes 17563648 | tf_op jit(solution)/shard_map/mac,maj->mcj/dot_general | solution.py:264
  113.5 0.3 all-to-all-done.3
  113.8 0.2 reshape.561
  114.2 0.5 fusion.1
  114.6 0.7 copy.54
  115.3 1.0 copy.56.depth_ref
  116.4 1.6 %copy-done = bf16[2,64,64,128]{3,2,1,0:T(8,128)(2,1)S(1)} copy-done((bf16[2,64,64,128]{3,2,1,0:T(8,128)(2,1)S(1)}, bf16[2,64,64,128]{3,2,1,0:T(8,128)(2,1)}, u32[]{:S(2)}) %copy-start) | copy-done | bytes 2097176
  118.0 4.4 %shard_map.77 = bf16[64,2,64,128]{3,2,1,0:T(8,128)(2,1)} custom-call(bf16[2,64,64,128]{3,2,1,0:T(8,128)(2,1)S(1)} %copy-done, bf16[2,64,64,32]{3,2,1,0:T(8,128)(2,1)S(1)} %copy.56.depth_ref, bf16[64,64]{1,0:T(8,128)(2,1)S(1)} %bitcast.191, bf16[32,128]{1,0:T(8,128)(2,1)S(1)} %copy-done.1), custom_call_target="tpu_custom_call" | custom-call | flops 201326592 | bytes 4194304 | tf_op jit(solution)/shard_map/pallas_call | solution.py:155
  (24 shorter events, 1.1 us)
Async XLA Ops:
  7.4 17.4 %all-to-all-start = ((bf16[16,64,128]{2,1,0:T(8,128)(2,1)}), bf16[16,64,128]{2,1,0:T(8,128)(2,1)S(1)}, u32[]{:S(2)}, u32[]{:S(2)}) async-start(bf16[16,64,128]{2,1,0:T(8,128)(2,1)} %reshape.548), calls=%async_computation | async-start | bytes 524288 | tf_op jit(solution)/shard_map/all_to_all | solution.py:72
  36.1 5.6 %copy-start.3 = (f32[64]{0:T(128)S(1)}, f32[64]{0:T(128)}, u32[]{:S(2)}) copy-start(f32[64]{0:T(128)} %param.9) | copy-start | bytes 772
  38.0 13.5 %all-to-all-start.1 = ((bf16[16,64,128]{2,1,0:T(8,128)(2,1)}), bf16[16,64,128]{2,1,0:T(8,128)(2,1)S(1)}, u32[]{:S(2)}, u32[]{:S(2)}) async-start(bf16[16,64,128]{2,1,0:T(8,128)(2,1)} %reshape.551), calls=%async_computation.1 | async-start | bytes 524288 | tf_op jit(solution)/shard_map/all_to_all | solution.py:72
  68.3 5.6 %copy-start.2 = (bf16[64,64]{1,0:T(8,128)(2,1)S(1)}, bf16[64,64]{1,0:T(8,128)(2,1)}, u32[]{:S(2)}) copy-start(bf16[64,64]{1,0:T(8,128)(2,1)} %weight_ref.1) | copy-start | bytes 24580
  70.3 13.5 %all-to-all-start.2 = ((bf16[16,64,128]{2,1,0:T(8,128)(2,1)}), bf16[16,64,128]{2,1,0:T(8,128)(2,1)S(1)}, u32[]{:S(2)}, u32[]{:S(2)}) async-start(bf16[16,64,128]{2,1,0:T(8,128)(2,1)} %reshape.556), calls=%async_computation.2 | async-start | bytes 524288 | tf_op jit(solution)/shard_map/all_to_all | solution.py:72
  100.3 13.5 %all-to-all-start.3 = ((bf16[16,64,128]{2,1,0:T(8,128)(2,1)}), bf16[16,64,128]{2,1,0:T(8,128)(2,1)S(1)}, u32[]{:S(2)}, u32[]{:S(2)}) async-start(bf16[16,64,128]{2,1,0:T(8,128)(2,1)} %reshape.560), calls=%async_computation.3 | async-start | bytes 524288 | tf_op jit(solution)/shard_map/all_to_all | solution.py:72
  115.3 1.1 copy-start.1
  116.4 1.6 %copy-start = (bf16[2,64,64,128]{3,2,1,0:T(8,128)(2,1)S(1)}, bf16[2,64,64,128]{3,2,1,0:T(8,128)(2,1)}, u32[]{:S(2)}) copy-start(bf16[2,64,64,128]{3,2,1,0:T(8,128)(2,1)} %get-tuple-element.7.up_ref) | copy-start | bytes 6291460
where the time goes:
time: 123 us; the launch traced here: 122 us
  matrix products  38.1 us (31%)
  waiting for transfers between devices  28.1 us (23%)
  starting transfers between devices  18.4 us (15%)
  local copies, waits for them, and re-layouts  17.1 us (14%)
  Pallas kernels  15.8 us (13%)
  other arithmetic  4.03 us (3%)
    all_to_all x4, waiting for transfers between devices, exchange(): return lax.all_to_all(blocks, 'gx', 0, 0, tiled=True)  28.1 us
    all_to_all x4, starting transfers between devices, exchange(): return lax.all_to_all(blocks, 'gx', 0, 0, tiled=True)  18.4 us
    dot_general x1, matrix products, body(): jnp.einsum('mcj,mbj->mbc', spectral_weight, pairs, preferred_element_type...  12.3 us
    pallas_call x1, Pallas kernels, middle(): pl.pallas_call(functools.partial(middle_kernel, scale), grid=(planes, lin...  11.4 us
    dot_general x1, matrix products, body(): jnp.einsum('mac,maj->mcj', coeffs, pairs, preferred_element_type=jnp.floa...  9.49 us
    dot_general x1, matrix products, mode_product(): jnp.einsum('mac,mcj->amj', coeffs, weights, preferred_element_type=jnp.fl...  8.14 us
    pallas_call x1, Pallas kernels, final(): pl.pallas_call(final_kernel, grid=(planes, lines // ROWS), in_specs=[pl.B...  4.42 us
    dot_general x1, matrix products, body(): jnp.dot(features, depth_basis.T, preferred_element_type=jnp.float32)  3.66 us
  transfers between devices with their start and end apart: 4, of which 4 were waited for; matrix products, arithmetic and copies ran while one was open for 9% of the time, Pallas kernels for 0%

commit v1 on v0

--- a/solution.py
+++ b/solution.py
@@ -51,12 +51,12 @@
 
 
 def gelu_parts(inputs):
-    cubed_in = inputs * inputs * inputs
-    tangent = jnp.tanh(SQRT_TWO_PI * (inputs + CUBIC_COEF * cubed_in))
-    output = 0.5 * inputs * (1.0 + tangent)
-    derivative = 0.5 * (1.0 + tangent) + 0.5 * inputs * (1.0 - tangent * tangent) * SQRT_TWO_PI * (
-        1.0 + 3.0 * CUBIC_COEF * inputs * inputs
-    )
+    squared = inputs * inputs
+    slope = SQRT_TWO_PI * CUBIC_COEF
+    tangent = jnp.tanh(inputs * (SQRT_TWO_PI + slope * squared))
+    half = 0.5 + 0.5 * tangent
+    output = inputs * half
+    derivative = half + output * (1.0 - tangent) * (SQRT_TWO_PI + 3.0 * slope * squared)
     return (output, derivative)
 
 

time: 123 us -> 123 us (level)
  no operation moved by 1% of the time
where the time goes in v1:
time: 123 us; the launch traced here: 122 us
  matrix products  38.1 us (31%)
  waiting for transfers between devices  28.1 us (23%)
  starting transfers between devices  18.4 us (15%)
  local copies, waits for them, and re-layouts  17.1 us (14%)
  Pallas kernels  15.4 us (13%)
  other arithmetic  4.03 us (3%)
    all_to_all x4, waiting for transfers between devices, exchange(): return lax.all_to_all(blocks, 'gx', 0, 0, tiled=True)  28.1 us
    all_to_all x4, starting transfers between devices, exchange(): return lax.all_to_all(blocks, 'gx', 0, 0, tiled=True)  18.4 us
    dot_general x1, matrix products, body(): jnp.einsum('mcj,mbj->mbc', spectral_weight, pairs, preferred_element_type...  12.3 us
    pallas_call x1, Pallas kernels, middle(): pl.pallas_call(functools.partial(middle_kernel, scale), grid=(planes, lin...  11 us
    dot_general x1, matrix products, body(): jnp.einsum('mac,maj->mcj', coeffs, pairs, preferred_element_type=jnp.floa...  9.49 us
    dot_general x1, matrix products, mode_product(): jnp.einsum('mac,mcj->amj', coeffs, weights, preferred_element_type=jnp.fl...  8.14 us
    pallas_call x1, Pallas kernels, final(): pl.pallas_call(final_kernel, grid=(planes, lines // ROWS), in_specs=[pl.B...  4.42 us
    dot_general x1, matrix products, body(): jnp.dot(features, depth_basis.T, preferred_element_type=jnp.float32)  3.66 us
  transfers between devices with their start and end apart: 4, of which 4 were waited for; matrix products, arithmetic and copies ran while one was open for 9% of the time, Pallas kernels for 0%

profile of v1, /device:TPU:0, one launch (start us, length us, event | category | flops | bytes accessed | tf_op | source)
XLA Modules:
  0.0 122.0 jit_solution(4302214794336831756)
XLA Ops:
  0.9 3.7 %convolution_convert_fusion = bf16[32,64,2,64]{3,0,2,1:T(8,128)(2,1)S(1)} fusion(bf16[64,2,64,128]{3,2,1,0:T(8,128)(2,1)} %feat_ref.1, bf16[16,128]{1,0:T(8,128)(2,1)S(1)} %get-tuple-element.35, bf16[16,128]{1,0:T(8,128)(2,1)S(1)} %get-tuple-element.36), kind=kOutput, calls=%fused_computation.3 | convolution fusion | flops 67387392 | bytes 2629632 | tf_op jit(solution)/shard_map/dot_general | solution.py:199
  4.5 1.4 %fusion.13 = bf16[32,16,2,2,64]{4,0,1,2,3:T(8,128)(2,1)S(1)} fusion(bf16[64,2,64,2,16]{2,4,3,1,0:T(8,128)(2,1)S(1)} %bitcast.196, bf16[64,1,2,32]{0,3,1,2:T(8,128)(2,1)S(1)} %get-tuple-element.22, bf16[64,1,2,32]{0,3,1,2:T(8,128)(2,1)S(1)} %get-tuple-element.21), kind=kOutput, calls=%fused_computation.25 | convolution fusion | flops 33718272 | bytes 802816 | tf_op jit(solution)/shard_map/cxyaz,yabk->kzxbc/dot_general | solution.py:202
  5.9 0.5 copy.29
  6.5 1.0 reshape.548
  7.4 7.4 %all-to-all-start = ((bf16[16,64,128]{2,1,0:T(8,128)(2,1)}), bf16[16,64,128]{2,1,0:T(8,128)(2,1)S(1)}, u32[]{:S(2)}, u32[]{:S(2)}) async-start(bf16[16,64,128]{2,1,0:T(8,128)(2,1)} %reshape.548), calls=%async_computation | async-start | bytes 524288 | tf_op jit(solution)/shard_map/all_to_all | solution.py:72
  15.0 0.2 negate_convert_fusion.2
  15.2 9.7 %all-to-all-done = bf16[16,64,128]{2,1,0:T(8,128)(2,1)S(1)} async-done(((bf16[16,64,128]{2,1,0:T(8,128)(2,1)}), bf16[16,64,128]{2,1,0:T(8,128)(2,1)S(1)}, u32[]{:S(2)}, u32[]{:S(2)}) %all-to-all-start) | async-done | bytes 262176 | tf_op jit(solution)/shard_map/all_to_all | solution.py:72
  24.8 0.2 reshape.549
  25.1 0.5 fusion.3
  25.6 8.1 %convolution_bitcast_fusion.5 = f32[2,1024,128]{2,0,1:T(2,128)S(1)} fusion(bf16[1024,64,128]{2,1,0:T(8,128)(2,1)} %param.7, bf16[1024,2,64]{2,0,1:T(8,128)(2,1)S(1)} %bitcast.199), kind=kOutput, calls=%fused_computation.11 | convolution fusion | flops 33554432 | bytes 18087936 | tf_op jit(solution)/shard_map/mac,mcj->amj/dot_general | solution.py:65
  33.7 2.3 %fusion.19 = (bf16[1,1024,64]{2,0,1:T(2,128)(2,1)S(1)}, bf16[1,1024,64]{2,0,1:T(2,128)(2,1)S(1)}) fusion(f32[2,1024,128]{2,0,1:T(2,128)S(1)} %convolution_bitcast_fusion.5), kind=kLoop, calls=%fused_computation.33 | loop fusion | flops 262144 | bytes 1310720 | tf_op jit(solution)/shard_map/convert.17
  36.2 0.3 fusion.11
  36.5 0.5 copy.34
  37.1 1.0 reshape.551
  38.0 3.7 %all-to-all-start.1 = ((bf16[16,64,128]{2,1,0:T(8,128)(2,1)}), bf16[16,64,128]{2,1,0:T(8,128)(2,1)S(1)}, u32[]{:S(2)}, u32[]{:S(2)}) async-start(bf16[16,64,128]{2,1,0:T(8,128)(2,1)} %reshape.551), calls=%async_computation.1 | async-start | bytes 524288 | tf_op jit(solution)/shard_map/all_to_all | solution.py:72
  41.8 0.7 copy.39.bias_ref
  42.5 0.6 pad_maximum_fusion.9.basis_ref
  43.2 8.4 %all-to-all-done.1 = bf16[16,64,128]{2,1,0:T(8,128)(2,1)S(1)} async-done(((bf16[16,64,128]{2,1,0:T(8,128)(2,1)}), bf16[16,64,128]{2,1,0:T(8,128)(2,1)S(1)}, u32[]{:S(2)}, u32[]{:S(2)}) %all-to-all-start.1) | async-done | bytes 262176 | tf_op jit(solution)/shard_map/all_to_all | solution.py:72
  51.6 0.2 reshape.552
  51.9 0.5 fusion
  52.4 0.7 copy.37
  53.1 1.8 %copy.38.lines_ref = bf16[2,64,64,32]{3,2,1,0:T(8,128)(2,1)} copy(bf16[2,64,64,32]{2,3,1,0:T(8,128)(2,1)S(1)} %bitcast.197) | data formatting | bytes 1048576 | tf_op jit(solution)/shard_map/reshape | solution.py:227
  54.9 11.0 %shard_map.76 = (bf16[64,2,64,128]{3,2,1,0:T(8,128)(2,1)}, bf16[2,64,64,128]{3,2,1,0:T(8,128)(2,1)}, bf16[2,64,64,32]{3,2,1,0:T(8,128)(2,1)}) custom-call(bf16[64,2,64,128]{3,2,1,0:T(8,128)(2,1)} %feat_ref.1, bf16[64,2,64,128]{3,2,1,0:T(8,128)(2,1)} %cot_ref.1, bf16[2,64,64,32]{3,2,1,0:T(8,128)(2,1)} %copy.38.lines_ref, bf16[64,64]{1,0:T(8,128)(2,1)} %weight_ref.1, ...), custom_call_target="tpu_custom_call" | custom-call | flops 268435456 | bytes 8388608 | tf_op jit(solution)/shard_map/pallas_call | solution.py:127
  65.9 2.0 %copy.40 = bf16[2,64,64,32]{2,3,1,0:T(8,128)(2,1)S(1)} copy(bf16[2,64,64,32]{3,2,1,0:T(8,128)(2,1)} %get-tuple-element.8) | data formatting | bytes 1048576 | tf_op jit(solution)/shard_map/pallas_call | solution.py:127
  67.9 0.5 fusion.12
  68.4 0.5 copy.43
  68.9 1.0 reshape.556
  69.9 3.5 %all-to-all-start.2 = ((bf16[16,64,128]{2,1,0:T(8,128)(2,1)}), bf16[16,64,128]{2,1,0:T(8,128)(2,1)S(1)}, u32[]{:S(2)}, u32[]{:S(2)}) async-start(bf16[16,64,128]{2,1,0:T(8,128)(2,1)} %reshape.556), calls=%async_computation.2 | async-start | bytes 524288 | tf_op jit(solution)/shard_map/all_to_all | solution.py:72
  73.5 0.2 fusion.96
  73.7 9.7 %all-to-all-done.2 = bf16[16,64,128]{2,1,0:T(8,128)(2,1)S(1)} async-done(((bf16[16,64,128]{2,1,0:T(8,128)(2,1)}), bf16[16,64,128]{2,1,0:T(8,128)(2,1)S(1)}, u32[]{:S(2)}, u32[]{:S(2)}) %all-to-all-start.2) | async-done | bytes 262176 | tf_op jit(solution)/shard_map/all_to_all | solution.py:72
  83.5 0.2 reshape.557
  83.7 0.5 fusion.5
  84.2 0.5 copy.45
  84.8 0.3 stack_reshape_reshape.4
  85.3 0.4 copy.47
  85.7 12.3 %fusion.7 = bf16[1024,2,64]{2,1,0:T(2,128)(2,1)S(1)} fusion(bf16[1024,64,128]{2,1,0:T(8,128)(2,1)} %param.7, bf16[1024,1,128]{2,1,0:T(2,128)(2,1)S(1)} %copy.47, bf16[1024,1,128]{2,1,0:T(2,128)(2,1)S(1)} %stack_reshape_reshape.4), kind=kOutput, calls=%fused_computation.19 | convolution fusion | flops 34865152 | bytes 17563648 | tf_op jit(solution)/shard_map/mcj,mbj->mbc/dot_general | solution.py:253
  98.0 0.3 fusion.10
  98.4 0.5 copy.50
  98.9 1.0 reshape.560
  99.9 3.8 %all-to-all-start.3 = ((bf16[16,64,128]{2,1,0:T(8,128)(2,1)}), bf16[16,64,128]{2,1,0:T(8,128)(2,1)S(1)}, u32[]{:S(2)}, u32[]{:S(2)}) async-start(bf16[16,64,128]{2,1,0:T(8,128)(2,1)} %reshape.560), calls=%async_computation.3 | async-start | bytes 524288 | tf_op jit(solution)/shard_map/all_to_all | solution.py:72
  103.6 9.5 %multiply_convert_fusion = bf16[1024,64,128]{2,1,0:T(8,128)(2,1)} fusion(bf16[1024,2,64]{2,0,1:T(8,128)(2,1)S(1)} %bitcast.200, bf16[1024,1,128]{2,1,0:T(2,128)(2,1)S(1)} %copy.47, bf16[1024,1,128]{2,1,0:T(2,128)(2,1)S(1)} %stack_reshape_reshape.4), kind=kOutput, calls=%fused_computation | convolution fusion | flops 51380224 | bytes 17563648 | tf_op jit(solution)/shard_map/mac,maj->mcj/dot_general | solution.py:264
  113.1 0.3 all-to-all-done.3
  113.4 0.2 reshape.561
  113.8 0.5 fusion.1
  114.2 0.7 copy.54
  114.9 1.0 copy.56.depth_ref
  116.0 1.6 %copy-done = bf16[2,64,64,128]{3,2,1,0:T(8,128)(2,1)S(1)} copy-done((bf16[2,64,64,128]{3,2,1,0:T(8,128)(2,1)S(1)}, bf16[2,64,64,128]{3,2,1,0:T(8,128)(2,1)}, u32[]{:S(2)}) %copy-start) | copy-done | bytes 2097176
  117.6 4.4 %shard_map.77 = bf16[64,2,64,128]{3,2,1,0:T(8,128)(2,1)} custom-call(bf16[2,64,64,128]{3,2,1,0:T(8,128)(2,1)S(1)} %copy-done, bf16[2,64,64,32]{3,2,1,0:T(8,128)(2,1)S(1)} %copy.56.depth_ref, bf16[64,64]{1,0:T(8,128)(2,1)S(1)} %bitcast.191, bf16[32,128]{1,0:T(8,128)(2,1)S(1)} %copy-done.1), custom_call_target="tpu_custom_call" | custom-call | flops 201326592 | bytes 4194304 | tf_op jit(solution)/shard_map/pallas_call | solution.py:155
  (24 shorter events, 1.1 us)
Async XLA Ops:
  7.4 17.4 %all-to-all-start = ((bf16[16,64,128]{2,1,0:T(8,128)(2,1)}), bf16[16,64,128]{2,1,0:T(8,128)(2,1)S(1)}, u32[]{:S(2)}, u32[]{:S(2)}) async-start(bf16[16,64,128]{2,1,0:T(8,128)(2,1)} %reshape.548), calls=%async_computation | async-start | bytes 524288 | tf_op jit(solution)/shard_map/all_to_all | solution.py:72
  36.1 5.6 %copy-start.3 = (f32[64]{0:T(128)S(1)}, f32[64]{0:T(128)}, u32[]{:S(2)}) copy-start(f32[64]{0:T(128)} %param.9) | copy-start | bytes 772
  38.0 13.5 %all-to-all-start.1 = ((bf16[16,64,128]{2,1,0:T(8,128)(2,1)}), bf16[16,64,128]{2,1,0:T(8,128)(2,1)S(1)}, u32[]{:S(2)}, u32[]{:S(2)}) async-start(bf16[16,64,128]{2,1,0:T(8,128)(2,1)} %reshape.551), calls=%async_computation.1 | async-start | bytes 524288 | tf_op jit(solution)/shard_map/all_to_all | solution.py:72
  67.9 5.6 %copy-start.2 = (bf16[64,64]{1,0:T(8,128)(2,1)S(1)}, bf16[64,64]{1,0:T(8,128)(2,1)}, u32[]{:S(2)}) copy-start(bf16[64,64]{1,0:T(8,128)(2,1)} %weight_ref.1) | copy-start | bytes 24580
  69.9 13.5 %all-to-all-start.2 = ((bf16[16,64,128]{2,1,0:T(8,128)(2,1)}), bf16[16,64,128]{2,1,0:T(8,128)(2,1)S(1)}, u32[]{:S(2)}, u32[]{:S(2)}) async-start(bf16[16,64,128]{2,1,0:T(8,128)(2,1)} %reshape.556), calls=%async_computation.2 | async-start | bytes 524288 | tf_op jit(solution)/shard_map/all_to_all | solution.py:72
  99.9 13.5 %all-to-all-start.3 = ((bf16[16,64,128]{2,1,0:T(8,128)(2,1)}), bf16[16,64,128]{2,1,0:T(8,128)(2,1)S(1)}, u32[]{:S(2)}, u32[]{:S(2)}) async-start(bf16[16,64,128]{2,1,0:T(8,128)(2,1)} %reshape.560), calls=%async_computation.3 | async-start | bytes 524288 | tf_op jit(solution)/shard_map/all_to_all | solution.py:72
  114.9 1.1 copy-start.1
  116.0 1.6 %copy-start = (bf16[2,64,64,128]{3,2,1,0:T(8,128)(2,1)S(1)}, bf16[2,64,64,128]{3,2,1,0:T(8,128)(2,1)}, u32[]{:S(2)}) copy-start(bf16[2,64,64,128]{3,2,1,0:T(8,128)(2,1)} %get-tuple-element.7.up_ref) | copy-start | bytes 6291460
